TPU v7x, 128 devices: a whole 4x4x4 slice. The times are simulated.
128 devices in a mesh: row: 16 (over z_hi, y, core), col: 8 (over x, z_lo).
Axes of the slice: x: 4, y: 4, z: 4 (z_hi: 2, z_lo: 2; z = z_hi * 2 + z_lo), core: 2. Of those that a mesh axis runs over, the one named last changes fastest.
Arguments:
- embeddings: bfloat16 [65536, 2560], P(('row', 'col')), may hold values from -6 to 6
- weight_in: bfloat16 [2560, 1024], replicated, may hold values from -0.125 to 0.125
- bias_in: float32 [1024], replicated, may hold values from -3 to 3
- weight_out: bfloat16 [1024, 64], replicated, may hold values from -0.1875 to 0.1875
- lengthscale: float32 [1], replicated, may hold values from 2 to 2.64
- noise_level: float32 [1], replicated, may hold values from 0.3 to 1
- right_side: float32 [33, 65536], P(None, ('row', 'col')), may hold values from -51 to 51
Outputs:
- residual: float32 [33, 65536], P(None, ('row', 'col'))
- direction: float32 [33, 65536], P(None, ('row', 'col'))
- step_size: float32 [33], replicated
- correction: float32 [33], replicated
All inputs are finite; a program needn't handle non-finite values.
Results may differ from a plain program's by a relative error of at most 0.0055.
Values may be sent and summed in bfloat16 or wider, within the bound.
A program may use at most 128 MiB of HBM per device.

v0:
```python
import math

import jax
import jax.numpy as jnp
from jax import lax
from jax.sharding import PartitionSpec as P


def tile_products_of(rows_feat, rows_norm, cols_feat, cols_probe, exponent_scale):
    cols_wide = cols_feat.astype(jnp.float32)
    cols_norm = jnp.sum(cols_wide * cols_wide, axis=0)
    width = rows_feat.shape[0]
    total_rows = rows_feat.shape[1]
    block_size = math.gcd(512, total_rows)
    block_count = total_rows // block_size
    feat_blocks = jnp.transpose(rows_feat.reshape(width, block_count, block_size), (1, 0, 2))
    norm_blocks = rows_norm.reshape(block_count, block_size)

    def tile_block(operand):
        feat_block, norm_block = operand
        inner = lax.dot_general(
            feat_block, cols_feat, (((0,), (0,)), ((), ())), preferred_element_type=jnp.float32
        )
        distance = norm_block[:, None] + cols_norm[None, :] - 2.0 * inner
        kernel = jnp.exp(-distance * exponent_scale).astype(jnp.bfloat16)
        return lax.dot_general(
            cols_probe, kernel, (((1,), (1,)), ((), ())), preferred_element_type=jnp.float32
        )

    pieces = lax.map(tile_block, (feat_blocks, norm_blocks))
    return jnp.transpose(pieces, (1, 0, 2)).reshape(cols_probe.shape[0], total_rows)


def norms_of(feat_half):
    wide = feat_half.astype(jnp.float32)
    return jnp.sum(wide * wide, axis=0)


def on_device(embeddings, weight_in, bias_in, weight_out, lengthscale, noise_level, right_side):
    hidden = jax.nn.gelu(
        jnp.dot(embeddings, weight_in, preferred_element_type=jnp.float32) + bias_in,
        approximate=False,
    ).astype(jnp.bfloat16)
    own_feat = lax.dot_general(
        weight_out, hidden, (((0,), (1,)), ((), ())), preferred_element_type=jnp.float32
    ).astype(jnp.bfloat16)
    exponent_scale = 0.5 / (lengthscale[0] * lengthscale[0])
    probe_half = right_side.astype(jnp.bfloat16)
    rows_dev = own_feat.shape[1]
    width = own_feat.shape[0]
    n_rowaxis = lax.axis_size("row")
    n_colaxis = lax.axis_size("col")
    all_feat = lax.all_gather(own_feat, ("row", "col"), axis=1, tiled=True)
    row_index = lax.axis_index("row")
    col_index = lax.axis_index("col")
    rows_feat = lax.dynamic_slice_in_dim(
        all_feat, row_index * (rows_dev * n_colaxis), rows_dev * n_colaxis, 1
    )
    grid_feat = all_feat.reshape(width, n_rowaxis, n_colaxis, rows_dev)
    cols_feat = lax.dynamic_index_in_dim(grid_feat, col_index, 2, keepdims=False).reshape(
        width, n_rowaxis * rows_dev
    )
    cols_probe = lax.all_gather(probe_half, "row", axis=1, tiled=True)
    partial_products = tile_products_of(
        rows_feat, norms_of(rows_feat), cols_feat, cols_probe, exponent_scale
    )
    images = (
        lax.psum_scatter(partial_products, "col", scatter_dimension=1, tiled=True)
        + noise_level[0] * right_side
    )
    local_old = jnp.sum(right_side * right_side, axis=1)
    local_curve = jnp.sum(right_side * images, axis=1)
    norm_old = lax.psum(local_old, ("row", "col"))
    curvature = lax.psum(local_curve, ("row", "col"))
    step_size = norm_old / curvature
    residual = right_side - step_size[:, None] * images
    norm_new = lax.psum(jnp.sum(residual * residual, axis=1), ("row", "col"))
    correction = norm_new / norm_old
    direction = residual + correction[:, None] * right_side
    return (residual, direction, step_size, correction)


def solution(mesh):
    in_specs = (P(("row", "col"), None), P(), P(), P(), P(), P(), P(None, ("row", "col")))
    out_specs = (P(None, ("row", "col")), P(None, ("row", "col")), P(), P())
    return jax.shard_map(
        on_device, mesh=mesh, in_specs=in_specs, out_specs=out_specs, check_vma=False
    )
```

profile of v0, /device:TPU:1, one launch (start us, length us, event | category | flops | bytes accessed | tf_op | source)
XLA Modules:
  0.0 594.1 jit_solution(1861877559295996428)
XLA Ops:
  7.2 0.0 all-gather.2.cloned.1.call-start
  7.2 1.7 copy-done
  8.9 10.3 %fusion.22 = bf16[64,512]{1,0:T(8,128)(2,1)} fusion(bf16[1024,64]{0,1:T(8,128)(2,1)} %param.12, bf16[512,2560]{1,0:T(8,128)(2,1)S(1)} %copy-done, bf16[2560,1024]{1,0:T(8,128)(2,1)} %param.10, f32[1024]{0:T(1024)} %param.11), kind=kOutput, calls=%fused_computation.31 | convolution fusion | flops 2786099200 | bytes 8065024 | tf_op jit(solution)/shard_map/dot_general | solution.py:44
  19.2 0.0 all-gather.2.cloned.1.call-update
  19.3 0.0 reduce-scatter.2.cloned.1.call-start
  20.0 29.8 %all_gather.7 = bf16[33,8192]{1,0:T(8,128)(2,1)} all-gather(bf16[33,512]{1,0:T(8,128)(2,1)S(1)} %convert_element_type.27), channel_id=1, replica_groups=mesh['row'=16,'col'=8] {'row'}, dimensions={1}, use_global_device_ids=true | all-gather | bytes 574464 | tf_op jit(solution)/shard_map/all_gather | solution.py:63
  49.8 286.6 %all-gather.2.cloned.1.call-done = bf16[64,65536]{1,0:T(8,128)(2,1)} async-done(((bf16[64,512]{1,0:T(8,128)(2,1)}), bf16[64,65536]{1,0:T(8,128)(2,1)}) %all-gather.2.cloned.1.call-update) | async-done | bytes 8388624 | tf_op jit(solution)/shard_map/all_gather | solution.py:53
  336.4 1.2 multiply_reduce_fusion.1
  337.6 9.9 %copy.16 = bf16[8,8,128,512]{3,2,1,0:T(8,128)(2,1)} copy(bf16[8,8,128,512]{3,1,2,0:T(8,128)(2,1)} %bitcast.50) | data formatting | bytes 16777216
  347.5 6.1 %constant_dynamic-slice_fusion.1 = bf16[64,16,1,512]{3,2,1,0:T(2,128)(2,1)S(1)} fusion(bf16[64,16,8,512]{3,2,1,0:T(8,128)(2,1)} %bitcast.49, s32[]{:T(128)S(6)} %select_n.8), kind=kLoop, calls=%fused_computation.70 | loop fusion | bytes 2097156 | tf_op jit(solution)/shard_map/jit(dynamic_index_in_dim)/dynamic_slice | solution.py:60
  353.6 0.4 multiply_reduce_fusion
  353.9 0.2 copy.18
  354.1 1.0 copy.13
  355.1 1.6 copy.19
  356.7 61.1 %while.10 = (s32[]{:T(128)}, f32[8,33,512]{2,1,0:T(8,128)S(1)}, f32[8,512]{1,0:T(8,128)S(1)}, f32[8192]{0:T(1024)S(1)}, bf16[8,64,512]{2,1,0:T(8,128)(2,1)}, /*i...) while((s32[]{:T(128)}, f32[8,33,512]{2,1,0:T(8,128)S(1)}, ...), condition=%wide.region_5.6_spmd, body=%wide.region_4.5_spmd.sunk | while | flops 838860800 | bytes 1891945 | solution.py:30
  356.7 7.6 %fusion.96 = f32[8,33,512]{2,1,0:T(8,128)S(1)} fusion(f32[8,33,512]{2,1,0:T(8,128)S(1)} %get-tuple-element.140, s32[]{:T(128)S(6)} %copy.25, bf16[33,8192]{1,0:T(8,128)(2,1)} %get-tuple-element.155, bf16[64,8192]{1,0:T(8,128)(2,1)} %get-tuple-element.153, f32[]{:T(128)} %get-tuple-element.154, f32[8192]{0:T(1024)S(1)} %get-tuple-element.151, ...), kind=kOutput, calls=%fused_computation.3.clone.1 | convolution fusion | flops 838860800 | bytes 1887744 | tf_op jit(solution)/shard_map/while/body/eval_jaxpr/dot_general | solution.py:26
  364.4 7.6 %fusion.96 = f32[8,33,512]{2,1,0:T(8,128)S(1)} fusion(f32[8,33,512]{2,1,0:T(8,128)S(1)} %get-tuple-element.140, s32[]{:T(128)S(6)} %copy.25, bf16[33,8192]{1,0:T(8,128)(2,1)} %get-tuple-element.155, bf16[64,8192]{1,0:T(8,128)(2,1)} %get-tuple-element.153, f32[]{:T(128)} %get-tuple-element.154, f32[8192]{0:T(1024)S(1)} %get-tuple-element.151, ...), kind=kOutput, calls=%fused_computation.3.clone.1 | convolution fusion | flops 838860800 | bytes 1887744 | tf_op jit(solution)/shard_map/while/body/eval_jaxpr/dot_general | solution.py:26
  372.0 7.6 %fusion.96 = f32[8,33,512]{2,1,0:T(8,128)S(1)} fusion(f32[8,33,512]{2,1,0:T(8,128)S(1)} %get-tuple-element.140, s32[]{:T(128)S(6)} %copy.25, bf16[33,8192]{1,0:T(8,128)(2,1)} %get-tuple-element.155, bf16[64,8192]{1,0:T(8,128)(2,1)} %get-tuple-element.153, f32[]{:T(128)} %get-tuple-element.154, f32[8192]{0:T(1024)S(1)} %get-tuple-element.151, ...), kind=kOutput, calls=%fused_computation.3.clone.1 | convolution fusion | flops 838860800 | bytes 1887744 | tf_op jit(solution)/shard_map/while/body/eval_jaxpr/dot_general | solution.py:26
  379.6 7.6 %fusion.96 = f32[8,33,512]{2,1,0:T(8,128)S(1)} fusion(f32[8,33,512]{2,1,0:T(8,128)S(1)} %get-tuple-element.140, s32[]{:T(128)S(6)} %copy.25, bf16[33,8192]{1,0:T(8,128)(2,1)} %get-tuple-element.155, bf16[64,8192]{1,0:T(8,128)(2,1)} %get-tuple-element.153, f32[]{:T(128)} %get-tuple-element.154, f32[8192]{0:T(1024)S(1)} %get-tuple-element.151, ...), kind=kOutput, calls=%fused_computation.3.clone.1 | convolution fusion | flops 838860800 | bytes 1887744 | tf_op jit(solution)/shard_map/while/body/eval_jaxpr/dot_general | solution.py:26
  387.3 7.6 %fusion.96 = f32[8,33,512]{2,1,0:T(8,128)S(1)} fusion(f32[8,33,512]{2,1,0:T(8,128)S(1)} %get-tuple-element.140, s32[]{:T(128)S(6)} %copy.25, bf16[33,8192]{1,0:T(8,128)(2,1)} %get-tuple-element.155, bf16[64,8192]{1,0:T(8,128)(2,1)} %get-tuple-element.153, f32[]{:T(128)} %get-tuple-element.154, f32[8192]{0:T(1024)S(1)} %get-tuple-element.151, ...), kind=kOutput, calls=%fused_computation.3.clone.1 | convolution fusion | flops 838860800 | bytes 1887744 | tf_op jit(solution)/shard_map/while/body/eval_jaxpr/dot_general | solution.py:26
  394.9 7.6 %fusion.96 = f32[8,33,512]{2,1,0:T(8,128)S(1)} fusion(f32[8,33,512]{2,1,0:T(8,128)S(1)} %get-tuple-element.140, s32[]{:T(128)S(6)} %copy.25, bf16[33,8192]{1,0:T(8,128)(2,1)} %get-tuple-element.155, bf16[64,8192]{1,0:T(8,128)(2,1)} %get-tuple-element.153, f32[]{:T(128)} %get-tuple-element.154, f32[8192]{0:T(1024)S(1)} %get-tuple-element.151, ...), kind=kOutput, calls=%fused_computation.3.clone.1 | convolution fusion | flops 838860800 | bytes 1887744 | tf_op jit(solution)/shard_map/while/body/eval_jaxpr/dot_general | solution.py:26
  402.6 7.6 %fusion.96 = f32[8,33,512]{2,1,0:T(8,128)S(1)} fusion(f32[8,33,512]{2,1,0:T(8,128)S(1)} %get-tuple-element.140, s32[]{:T(128)S(6)} %copy.25, bf16[33,8192]{1,0:T(8,128)(2,1)} %get-tuple-element.155, bf16[64,8192]{1,0:T(8,128)(2,1)} %get-tuple-element.153, f32[]{:T(128)} %get-tuple-element.154, f32[8192]{0:T(1024)S(1)} %get-tuple-element.151, ...), kind=kOutput, calls=%fused_computation.3.clone.1 | convolution fusion | flops 838860800 | bytes 1887744 | tf_op jit(solution)/shard_map/while/body/eval_jaxpr/dot_general | solution.py:26
  410.2 7.6 %fusion.96 = f32[8,33,512]{2,1,0:T(8,128)S(1)} fusion(f32[8,33,512]{2,1,0:T(8,128)S(1)} %get-tuple-element.140, s32[]{:T(128)S(6)} %copy.25, bf16[33,8192]{1,0:T(8,128)(2,1)} %get-tuple-element.155, bf16[64,8192]{1,0:T(8,128)(2,1)} %get-tuple-element.153, f32[]{:T(128)} %get-tuple-element.154, f32[8192]{0:T(1024)S(1)} %get-tuple-element.151, ...), kind=kOutput, calls=%fused_computation.3.clone.1 | convolution fusion | flops 838860800 | bytes 1887744 | tf_op jit(solution)/shard_map/while/body/eval_jaxpr/dot_general | solution.py:26
  417.8 0.3 copy.14
  418.2 0.1 pad
  418.2 1.2 copy.20
  420.1 32.2 %reduce-scatter.2.cloned.1.call-done = f32[33,512]{1,0:T(8,128)} async-done(((f32[33,4096]{1,0:T(8,128)}), f32[33,512]{1,0:T(8,128)}) %reduce-scatter.2.cloned.1.call-update) | async-done | bytes 67600 | tf_op jit(solution)/shard_map/reduce_scatter | solution.py:68
  452.3 1.0 multiply_reduce_fusion.3
  453.3 68.0 %all-reduce = (f32[33]{0:T(128)S(1)}, f32[33]{0:T(128)S(1)}) all-reduce(f32[33]{0:T(128)S(1)} %get-tuple-element.56, f32[33]{0:T(128)S(1)} %get-tuple-element.55), channel_id=1, replica_groups=mesh['row'=16,'col'=8] {'row','col'}, use_global_device_ids=true, to_apply=%region_1.2 | all-reduce | flops 66 | bytes 528 | tf_op jit(solution)/shard_map/psum | solution.py:73
  521.4 1.1 multiply_reduce_fusion.2
  522.5 64.1 %psum.23 = f32[33]{0:T(128)S(1)} all-reduce(f32[33]{0:T(128)S(1)} %get-tuple-element.75), channel_id=1, replica_groups=mesh['row'=16,'col'=8] {'row','col'}, use_global_device_ids=true, to_apply=%region_10.11 | all-reduce | flops 33 | bytes 264 | tf_op jit(solution)/shard_map/psum | solution.py:77
  586.6 0.7 multiply_add_fusion
  (26 shorter events, 0.1 us)
Async XLA Ops:
  7.2 1.7 copy-start
  7.2 12.8 %copy-start.1 = (f32[33,512]{1,0:T(8,128)S(1)}, f32[33,512]{1,0:T(8,128)}, u32[]{:S(2)}) copy-start(f32[33,512]{1,0:T(8,128)} %param.15) | copy-start | bytes 202756
  7.2 329.2 %all-gather.2.cloned.1.call-start = ((), (), s32[]{:S(2)}) async-start(), calls=%async_computation.1 | async-start | bytes 8454144 | tf_op jit(solution)/shard_map/all_gather | solution.py:53
  19.3 433.1 %reduce-scatter.2.cloned.1.call-start = ((), (), s32[]{:S(2)}) async-start(), calls=%async_computation.2 | async-start | bytes 737280 | tf_op jit(solution)/shard_map/reduce_scatter | solution.py:68
  354.1 2.6 copy-start.2
  521.4 65.9 %copy-start.4 = (f32[33]{0:T(128)}, f32[33]{0:T(128)S(1)}, u32[]{:S(2)}) copy-start(f32[33]{0:T(128)S(1)} %div.14) | copy-start | bytes 400
  522.5 64.8 %copy-start.3 = (f32[33,512]{1,0:T(8,128)}, f32[33,512]{1,0:T(8,128)S(1)}, u32[]{:S(2)}) copy-start(f32[33,512]{1,0:T(8,128)S(1)} %get-tuple-element.76) | copy-start | bytes 202756
  586.6 0.7 copy-start.5
Sparse Core Ops, SparseCore 0:
  19.4 316.9 all-gather.1
  419.6 32.7 reduce-scatter.1
where the time goes:
time: 595 us; the launch traced here: 594 us
  waiting for transfers between devices  319 us (54%)
  blocking collectives  162 us (27%)
  matrix products  71.2 us (12%)
  local copies, waits for them, and re-layouts  22.1 us (4%)
  between operations  15.5 us (3%)
    all_gather x1, waiting for transfers between devices, on_device(): all_feat = lax.all_gather(own_feat, ('row', 'col'), axis=1, tiled=True)  287 us
    psum x1, blocking collectives, on_device(): norm_old = lax.psum(local_old, ('row', 'col'))  68 us
    psum x1, blocking collectives, on_device(): norm_new = lax.psum(jnp.sum(residual * residual, axis=1), ('row', 'col'))  64.1 us
    dot_general x8, matrix products, tile_block(): lax.dot_general(cols_probe, kernel, (((1,), (1,)), ((), ())), preferred_e...  60.9 us
    reduce_scatter x1, waiting for transfers between devices, on_device(): lax.psum_scatter(partial_products, 'col', scatter_dimension=1, tiled=True)  32.2 us
    all_gather x1, blocking collectives, on_device(): cols_probe = lax.all_gather(probe_half, 'row', axis=1, tiled=True)  29.8 us
    unnamed x18, local copies, waits for them, and re-layouts  14.6 us
  transfers between devices with their start and end apart: 2, of which 2 were waited for; matrix products, arithmetic and copies ran while one was open for 0% of the time, Pallas kernels for 0%

commit v1 on v0

v1 whole, which is shorter than its diff:
```python
import functools
import math

import jax
import jax.numpy as jnp
from jax import lax
from jax.experimental import pallas as pl
from jax.experimental.pallas import tpu as pltpu
from jax.sharding import PartitionSpec as P

MESH = pl.DeviceIdType.MESH
F32 = jnp.float32
BF16 = jnp.bfloat16

LINES = 16
MEMBERS = 8
BLOCK = 512
HALF = 256
SPAN = MEMBERS * HALF
FEAT = 64
EMBED = 2560
INNER = 1024
COLS = 33
PROBE_ROWS = 48
SUM_ROWS = 40
STRIP = 1024
SUB = 512
NCHUNK = 256


def device_of(line, member):
    y, z = line // 4, line % 4
    x, core = member // 2, member % 2
    return ((z // 2) * 8 + y * 2 + core, x * 2 + z % 2)


def gelu(v):
    return 0.5 * v * (1.0 + lax.erf(v * (1.0 / math.sqrt(2.0))))


def pieces_of(v):
    first = v.astype(BF16).astype(F32)
    rest = v - first
    second = rest.astype(BF16).astype(F32)
    third = (rest - second).astype(BF16).astype(F32)
    return first, second, third


def kernel(
    emb, w_in, bias, w_out, scale_in, noise_in, rs_in,
    img_out, sc_out,
    x_buf, w_buf, b_buf, wo_buf, rs_buf, rs_pad, p_own, probes, feats, at, bb,
    acc_a, acc_b, parts, stat_own, stat_line, stat_mid, stat_all,
    load_sem, ps_sem, pr_sem, fs_sem, fr_sem, qs_sem, qr_sem, s1_sem, r1_sem, s2_sem, r2_sem,
):
    row, col = lax.axis_index("row"), lax.axis_index("col")
    line = ((row // 2) % 4) * 4 + (row // 8) * 2 + col % 2
    member = (col // 2) * 2 + row % 2
    b_line = (line + member + 1) % LINES

    def mate(j):
        return (member + j) % MEMBERS

    def target(k):
        return device_of((line + LINES - k) % LINES, k - 1)

    loads = []

    def load(src, dst):
        c = pltpu.make_async_copy(src, dst, load_sem.at[len(loads)])
        c.start()
        loads.append(c)
        return c

    load_rs = load(rs_in, rs_buf)
    load_x = [load(emb.at[pl.ds(0, HALF), :], x_buf.at[0])]
    load_w = [
        load(w_in.at[:, pl.ds(n * NCHUNK, NCHUNK)], w_buf.at[n]) for n in range(INNER // NCHUNK)
    ]
    load_b = load(bias, b_buf)
    load_wo = load(w_out, wo_buf)
    load_x.append(load(emb.at[pl.ds(HALF, HALF), :], x_buf.at[1]))

    barrier = pltpu.get_barrier_semaphore()

    def greet(device):
        pl.semaphore_signal(barrier, inc=1, device_id=device, device_id_type=MESH)

    @pl.loop(1, MEMBERS)
    def _(j):
        greet(device_of(line, mate(j)))

    @pl.loop(0, MEMBERS)
    def _(j):
        greet(target(j + 1))
        greet(device_of(b_line, j))

    @pl.loop(1, LINES)
    def _(j):
        greet(device_of((line + j) % LINES, member))

    load_rs.wait()
    rs_pad[...] = jnp.zeros_like(rs_pad)
    rs_pad[pl.ds(0, COLS), :] = rs_buf[...]
    for h in range(2):
        p_own[h] = rs_pad[:, pl.ds(h * HALF, HALF)].astype(BF16)
    own = pl.ds(pl.multiple_of(member * HALF, HALF), HALF)
    for h in range(2):
        probes[2 + h, :, own] = p_own[h]

    acc_a[...] = jnp.zeros_like(acc_a)
    acc_b[...] = jnp.zeros_like(acc_b)

    pl.semaphore_wait(barrier, 7 + 8 + 8 + 15)

    def probe_copy(base, sem_at, recv_at, device):
        return pltpu.make_async_remote_copy(
            src_ref=p_own,
            dst_ref=probes.at[pl.ds(base, 2), :, own],
            send_sem=ps_sem.at[sem_at],
            recv_sem=pr_sem.at[recv_at],
            device_id=device,
            device_id_type=MESH,
        )

    @pl.loop(1, MEMBERS)
    def _(j):
        probe_copy(2, j, member, device_of(line, mate(j))).start()

    @pl.loop(0, MEMBERS)
    def _(j):
        probe_copy(0, MEMBERS + j, MEMBERS + member, target(j + 1)).start()

    def feat_copy(h, base, sem_at, recv_at, device):
        return pltpu.make_async_remote_copy(
            src_ref=feats.at[2 + h, :, own],
            dst_ref=feats.at[base + h, :, own],
            send_sem=fs_sem.at[h, sem_at],
            recv_sem=fr_sem.at[h, recv_at],
            device_id=device,
            device_id_type=MESH,
        )

    for h in range(2):
        load_x[h].wait()
        total = jnp.zeros((HALF, FEAT), F32)
        for n in range(INNER // NCHUNK):
            if h == 0:
                load_w[n].wait()
                if n == 0:
                    load_b.wait()
                    load_wo.wait()
            pre = jnp.dot(x_buf[h], w_buf[n], preferred_element_type=F32)
            hidden = gelu(pre + b_buf[:, pl.ds(n * NCHUNK, NCHUNK)]).astype(BF16)
            total += jnp.dot(
                hidden, wo_buf[pl.ds(n * NCHUNK, NCHUNK), :], preferred_element_type=F32
            )
        feats[2 + h, :, own] = total.T.astype(BF16)

        @pl.loop(1, MEMBERS)
        def _(j):
            feat_copy(h, 2, j, member, device_of(line, mate(j))).start()

        @pl.loop(0, MEMBERS)
        def _(j):
            feat_copy(h, 0, MEMBERS + j, MEMBERS + member, target(j + 1)).start()

    length = jnp.full((1, SPAN), scale_in[0], F32)
    unit = (1.0 / math.log(2.0)) / (length * length)
    level = lax.broadcasted_iota(jnp.int32, (FEAT, SPAN), 0)

    def extras(norm, at_norm, at_one):
        one, two, three = pieces_of(norm)
        out = jnp.where((level >= at_one) & (level < at_one + 3), 1.0, 0.0)
        for i, piece in enumerate((one, two, three)):
            out = jnp.where(level == at_norm + i, jnp.broadcast_to(piece, out.shape), out)
        return out

    def build_columns(half):
        wide = feats[half].astype(F32)
        norm = jnp.sum(wide * wide, axis=0, keepdims=True) * (unit * -0.5)
        for i, piece in enumerate(pieces_of(wide * unit)):
            bb[half, pl.ds(i * FEAT, FEAT), :] = piece.astype(BF16)
        bb[half, pl.ds(3 * FEAT, FEAT), :] = extras(norm, 0, 3).astype(BF16)

    def build_rows(h):
        wide = feats[2 + h].astype(F32)
        norm = jnp.sum(wide * wide, axis=0, keepdims=True) * (unit * -0.5)
        at[h, :, pl.ds(0, 128)] = jnp.concatenate([wide, wide], axis=0).T.astype(BF16)
        at[h, :, pl.ds(128, 128)] = jnp.concatenate([wide, extras(norm, 3, 0)], axis=0).T.astype(BF16)

    def wait_half(h):
        @pl.loop(1, MEMBERS)
        def _(j):
            feat_copy(h, 2, j, mate(j), device_of(line, mate(j))).wait_recv()

        @pl.loop(0, MEMBERS)
        def _(j):
            feat_copy(h, 0, j, MEMBERS + j, device_of(b_line, j)).wait_recv()

    def strip(a, b, at_col, both):
        cols = bb[b, :, pl.ds(at_col, STRIP)]
        down = jnp.zeros((PROBE_ROWS, STRIP), F32)
        for i in range(SPAN // SUB):
            rows = pl.ds(i * SUB, SUB)
            power = jnp.dot(at[a, rows, :], cols, preferred_element_type=F32)
            tile = jnp.exp2(power).astype(BF16)
            down += jnp.dot(probes[2 + a, :, rows], tile, preferred_element_type=F32)
            if both:
                acc_a[a, :, rows] += lax.dot_general(
                    probes[b, :, pl.ds(at_col, STRIP)], tile, (((1,), (1,)), ((), ())),
                    preferred_element_type=F32,
                )
        acc_b[b, :, pl.ds(at_col, STRIP)] += down

    def quad(a, b, both):
        @pl.loop(0, SPAN // STRIP)
        def _(i):
            strip(a, b, pl.multiple_of(i * STRIP, STRIP), both)

    @pl.loop(1, MEMBERS)
    def _(j):
        probe_copy(2, j, mate(j), device_of(line, mate(j))).wait_recv()

    @pl.loop(0, MEMBERS)
    def _(j):
        probe_copy(0, j, MEMBERS + j, device_of(b_line, j)).wait_recv()

    wait_half(0)
    build_rows(0)
    build_columns(0)

    @pl.when(member < 7)
    def _():
        quad(0, 0, True)

    @pl.when(member == 7)
    def _():
        build_columns(2)
        quad(0, 2, False)

    wait_half(1)
    build_rows(1)
    build_columns(1)

    @pl.when(member == 7)
    def _():
        build_columns(3)
        quad(1, 3, False)

    last = member // 7
    w = line // 8

    @pl.loop(0, 3)
    def _(t):
        second, third = t % 2, t // 2
        is_first = (2 - t) // 2
        a_pair = 1 - is_first
        b_pair = 1 - third
        a_last = second
        b_last = is_first * w + second * (1 - w) + third * 3
        quad(a_pair * (1 - last) + a_last * last, b_pair * (1 - last) + b_last * last, True)

    @pl.when(member == 7)
    def _():
        for h in range(2):
            acc_a[h] += acc_b[2 + h]

    def part_copy(kind, block, sem_at, recv_at, device):
        src = (acc_a, acc_b)[kind]
        return pltpu.make_async_remote_copy(
            src_ref=src.at[
                pl.ds(0, 2), pl.ds(0, SUM_ROWS), pl.ds(pl.multiple_of(block * HALF, HALF), HALF)
            ],
            dst_ref=parts.at[recv_at],
            send_sem=qs_sem.at[sem_at],
            recv_sem=qr_sem.at[recv_at],
            device_id=device,
            device_id_type=MESH,
        )

    @pl.loop(0, MEMBERS)
    def _(j):
        part_copy(1, j, MEMBERS + j, MEMBERS + member, device_of(b_line, j)).start()

    @pl.loop(1, MEMBERS)
    def _(j):
        part_copy(0, mate(j), j, member, device_of(line, mate(j))).start()

    images = [
        acc_a[h, pl.ds(0, SUM_ROWS), own]
        + noise_in[0] * rs_pad[pl.ds(0, SUM_ROWS), pl.ds(h * HALF, HALF)]
        for h in range(2)
    ]

    @pl.loop(1, MEMBERS)
    def _(j):
        part_copy(0, mate(j), j, mate(j), device_of(line, mate(j))).wait_recv()

    @pl.loop(0, MEMBERS)
    def _(j):
        part_copy(1, j, j, MEMBERS + j, target(j + 1)).wait_recv()

    parts[member] = jnp.zeros((2, SUM_ROWS, HALF), F32)
    for h in range(2):
        images[h] = images[h] + jnp.sum(parts[:, h], axis=0)
        img_out[:, pl.ds(h * HALF, HALF)] = images[h][:COLS]

    right = [rs_pad[pl.ds(0, SUM_ROWS), pl.ds(h * HALF, HALF)] for h in range(2)]

    def over(terms):
        return sum(jnp.sum(t, axis=1, keepdims=True) for t in terms)

    def ratio(top, bottom):
        return jnp.where(bottom > 0.0, top / jnp.where(bottom > 0.0, bottom, 1.0), 0.0)

    norm = over([r * r for r in right])
    curve = over([r * i for r, i in zip(right, images)])
    alpha = ratio(curve, norm)
    spread = over([(i - alpha * r) * (i - alpha * r) for r, i in zip(right, images)])
    lane = lax.broadcasted_iota(jnp.int32, (SUM_ROWS, 128), 1)

    def packed(values):
        out = jnp.zeros((SUM_ROWS, 128), F32)
        for i, v in enumerate(values):
            out = jnp.where(lane == i, jnp.broadcast_to(v, out.shape), out)
        return out

    def merged(stats):
        norms, curves, spreads = (stats[:, :, i : i + 1] for i in range(3))
        norm = jnp.sum(norms, axis=0)
        curve = jnp.sum(curves, axis=0)
        shift = ratio(curves, norms) - ratio(curve, norm)[None]
        return norm, curve, jnp.sum(spreads + norms * shift * shift, axis=0)

    stat_own[...] = packed((norm, curve, spread))

    def line_copy(sem_at, recv_at, device):
        return pltpu.make_async_remote_copy(
            src_ref=stat_own, dst_ref=stat_line.at[recv_at],
            send_sem=s1_sem.at[sem_at], recv_sem=r1_sem.at[recv_at],
            device_id=device, device_id_type=MESH,
        )

    @pl.loop(1, MEMBERS)
    def _(j):
        line_copy(j, member, device_of(line, mate(j))).start()

    @pl.loop(1, MEMBERS)
    def _(j):
        line_copy(j, mate(j), device_of(line, mate(j))).wait_recv()

    stat_line[member] = stat_own[...]
    stat_mid[...] = packed(merged(stat_line[...]))

    def across(j):
        return (line + j) % LINES

    def all_copy(sem_at, recv_at, device):
        return pltpu.make_async_remote_copy(
            src_ref=stat_mid, dst_ref=stat_all.at[recv_at],
            send_sem=s2_sem.at[sem_at], recv_sem=r2_sem.at[recv_at],
            device_id=device, device_id_type=MESH,
        )

    @pl.loop(1, LINES)
    def _(j):
        all_copy(j, line, device_of(across(j), member)).start()

    @pl.loop(1, LINES)
    def _(j):
        all_copy(j, across(j), device_of(across(j), member)).wait_recv()

    stat_all[line] = stat_mid[...]
    norm, curve, spread = merged(stat_all[...])
    step = norm / curve
    sc_out[...] = packed((step, step * step * spread / norm))[:COLS]

    @pl.loop(1, MEMBERS)
    def _(j):
        there = device_of(line, mate(j))
        probe_copy(2, j, member, there).wait_send()
        feat_copy(0, 2, j, member, there).wait_send()
        feat_copy(1, 2, j, member, there).wait_send()
        part_copy(0, mate(j), j, member, there).wait_send()
        line_copy(j, member, there).wait_send()

    @pl.loop(0, MEMBERS)
    def _(j):
        there = target(j + 1)
        probe_copy(0, MEMBERS + j, MEMBERS + member, there).wait_send()
        feat_copy(0, 0, MEMBERS + j, MEMBERS + member, there).wait_send()
        feat_copy(1, 0, MEMBERS + j, MEMBERS + member, there).wait_send()
        part_copy(1, j, MEMBERS + j, MEMBERS + member, device_of(b_line, j)).wait_send()

    @pl.loop(1, LINES)
    def _(j):
        all_copy(j, line, device_of(across(j), member)).wait_send()


def on_device(embeddings, weight_in, bias_in, weight_out, lengthscale, noise_level, right_side):
    anywhere = pl.BlockSpec(memory_space=pl.ANY)
    scalar = pl.BlockSpec(memory_space=pltpu.SMEM)
    vmem = pl.BlockSpec(memory_space=pltpu.VMEM)
    dma = pltpu.SemaphoreType.DMA
    images, scalars = pl.pallas_call(
        kernel,
        out_shape=(
            jax.ShapeDtypeStruct((COLS, BLOCK), F32),
            jax.ShapeDtypeStruct((COLS, 128), F32),
        ),
        in_specs=[anywhere, anywhere, anywhere, anywhere, scalar, scalar, anywhere],
        out_specs=[vmem, vmem],
        scratch_shapes=[
            pltpu.VMEM((2, HALF, EMBED), BF16),
            pltpu.VMEM((INNER // NCHUNK, EMBED, NCHUNK), BF16),
            pltpu.VMEM((1, INNER), F32),
            pltpu.VMEM((INNER, FEAT), BF16),
            pltpu.VMEM((COLS, BLOCK), F32),
            pltpu.VMEM((PROBE_ROWS, BLOCK), F32),
            pltpu.VMEM((2, PROBE_ROWS, HALF), BF16),
            pltpu.VMEM((4, PROBE_ROWS, SPAN), BF16),
            pltpu.VMEM((4, FEAT, SPAN), BF16),
            pltpu.VMEM((2, SPAN, 256), BF16),
            pltpu.VMEM((4, 256, SPAN), BF16),
            pltpu.VMEM((2, PROBE_ROWS, SPAN), F32),
            pltpu.VMEM((4, PROBE_ROWS, SPAN), F32),
            pltpu.VMEM((2 * MEMBERS, 2, SUM_ROWS, HALF), F32),
            pltpu.VMEM((SUM_ROWS, 128), F32),
            pltpu.VMEM((MEMBERS, SUM_ROWS, 128), F32),
            pltpu.VMEM((SUM_ROWS, 128), F32),
            pltpu.VMEM((LINES, SUM_ROWS, 128), F32),
            dma((9,)),
            dma((2 * MEMBERS,)),
            dma((2 * MEMBERS,)),
            dma((2, 2 * MEMBERS)),
            dma((2, 2 * MEMBERS)),
            dma((2 * MEMBERS,)),
            dma((2 * MEMBERS,)),
            dma((MEMBERS,)),
            dma((MEMBERS,)),
            dma((LINES,)),
            dma((LINES,)),
        ],
        compiler_params=pltpu.CompilerParams(
            collective_id=0, has_side_effects=True, vmem_limit_bytes=56 * 2**20
        ),
        name="cg_step",
    )(
        embeddings, weight_in, bias_in.reshape(1, INNER), weight_out, lengthscale, noise_level,
        right_side,
    )
    step_size = scalars[:, 0]
    correction = scalars[:, 1]
    residual = right_side - step_size[:, None] * images
    direction = residual + correction[:, None] * right_side
    return (residual, direction, step_size, correction)


def solution(mesh):
    in_specs = (P(("row", "col"), None), P(), P(), P(), P(), P(), P(None, ("row", "col")))
    out_specs = (P(None, ("row", "col")), P(None, ("row", "col")), P(), P())
    return jax.shard_map(
        on_device, mesh=mesh, in_specs=in_specs, out_specs=out_specs, check_vma=False
    )
```

time: 595 us -> 96.2 us (0.16)
  waiting for transfers between devices: 319 us -> 0 us
  blocking collectives: 162 us -> 0 us
  Pallas kernels: 0 us -> 89.1 us
  matrix products: 71.2 us -> 0 us
  local copies, waits for them, and re-layouts: 22.1 us -> 2.74 us
  between operations: 15.5 us -> 2 us
    all_gather x1 -> x0, waiting for transfers between devices: 287 us -> none  [on_device(): all_feat = lax.all_gather(own_feat, ('row', 'col'), axis=1, tiled=True)]
    psum x2 -> x0, blocking collectives: 132 us -> none  [the longest x1 68 us: on_device(): norm_old = lax.psum(local_old, ('row', 'col'))]
    pallas_call x0 -> x1, Pallas kernels: none -> 89.1 us  [on_device(): pl.pallas_call(kernel, out_shape=(jax.ShapeDtypeStruct((COLS, BLOCK), F32...]
    dot_general x9 -> x0, matrix products: 71.2 us -> none  [the longest x8 60.9 us: tile_block(): lax.dot_general(cols_probe, kernel, (((1,), (1,)), ((), ())), preferred_e...]
    reduce_scatter x1 -> x0, waiting for transfers between devices: 32.2 us -> none  [on_device(): lax.psum_scatter(partial_products, 'col', scatter_dimension=1, tiled=True)]
    all_gather x1 -> x0, blocking collectives: 29.8 us -> none  [on_device(): cols_probe = lax.all_gather(probe_half, 'row', axis=1, tiled=True)]
    unnamed x18 -> x7, local copies, waits for them, and re-layouts: 14.6 us -> 1.76 us
    dynamic_slice x9 -> x0, local copies, waits for them, and re-layouts: 6.15 us -> none  [the longest x1 6.08 us: on_device(): lax.dynamic_index_in_dim(grid_feat, col_index, 2, keepdims=False)]
  transfers between devices with their start and end apart: 2 -> 0, of which waited for: 2 -> 0; matrix products, arithmetic and copies ran while one was open for 0% -> 0% of each run, Pallas kernels for 0% -> 0%
where the time goes in v1:
time: 96.2 us; the launch traced here: 95.5 us
  Pallas kernels  89.1 us (93%)
  local copies, waits for them, and re-layouts  2.74 us (3%)
  between operations  2 us (2%)
  other arithmetic  1.63 us (2%)
    pallas_call x1, Pallas kernels, on_device(): pl.pallas_call(kernel, out_shape=(jax.ShapeDtypeStruct((COLS, BLOCK), F32...  89.1 us

profile of v1, /device:TPU:1, one launch (start us, length us, event | category | flops | bytes accessed | tf_op | source)
XLA Modules:
  0.0 95.5 jit_solution(13480621756806904539)
XLA Ops:
  0.6 0.0 copy-start
  2.0 1.7 %copy.12.w_out = bf16[1024,64]{1,0:T(8,128)(2,1)} copy(bf16[1024,64]{0,1:T(8,128)(2,1)} %param.10) | data formatting | bytes 262144 | tf_op args[3]
  3.7 89.1 %cg_step.1 = (f32[33,512]{1,0:T(8,128)}, f32[33,128]{1,0:T(8,128)}) custom-call(bf16[512,2560]{1,0:T(8,128)(2,1)} %emb.1, bf16[2560,1024]{1,0:T(8,128)(2,1)} %w_in.1, f32[1,1024]{1,0:T(1,128)} %bitcast.1, bf16[1024,64]{1,0:T(8,128)(2,1)} %copy.12.w_out, f32[1]{0:T(128)S(6)} %copy.13.scale_in, f32[1]{0:T(128)S(6)} %copy.14.noise_in, f32[33,512]{1,0:T(8,128)} %rs_in.1), custom_call_target="tpu_custom_call" | custom-call | tf_op jit(solution)/shard_map/cg_step/pallas_call | solution.py:406
  92.8 1.0 %slice_reduce_fusion = (f32[33]{0:T(128)S(1)}, f32[33]{0:T(128)S(1)}) fusion(f32[33,128]{1,0:T(8,128)} %get-tuple-element.6), kind=kLoop, calls=%fused_computation.2 | loop fusion | bytes 528 | tf_op jit(solution)/shard_map/slice | solution.py:454
  93.8 0.0 copy-start.1
  93.8 0.0 copy-start.2
  93.9 0.0 copy-done
  93.9 1.6 %multiply_add_fusion = (f32[33,512]{1,0:T(8,128)}, f32[33,512]{1,0:T(8,128)}) fusion(f32[33,512]{1,0:T(8,128)S(1)} %copy-done, f32[33]{0:T(128)S(1)} %get-tuple-element.8, f32[33,512]{1,0:T(8,128)} %get-tuple-element.7, f32[33]{0:T(128)S(1)} %get-tuple-element.9), kind=kLoop, calls=%fused_computation | loop fusion | flops 67584 | bytes 270600 | tf_op jit(solution)/shard_map/add | solution.py:456
  95.5 0.0 copy-done.1
  95.5 0.0 copy-done.2
Async XLA Ops:
  0.6 93.2 %copy-start = (f32[33,512]{1,0:T(8,128)S(1)}, f32[33,512]{1,0:T(8,128)}, u32[]{:S(2)}) copy-start(f32[33,512]{1,0:T(8,128)} %rs_in.1) | copy-start | bytes 202756
  93.8 1.7 %copy-start.1 = (f32[33]{0:T(128)}, f32[33]{0:T(128)S(1)}, u32[]{:S(2)}) copy-start(f32[33]{0:T(128)S(1)} %get-tuple-element.8) | copy-start | bytes 400
  93.8 1.7 %copy-start.2 = (f32[33]{0:T(128)}, f32[33]{0:T(128)S(1)}, u32[]{:S(2)}) copy-start(f32[33]{0:T(128)S(1)} %get-tuple-element.9) | copy-start | bytes 400

commit v2 on v0

v2 whole, which is shorter than its diff:
```python
import functools
import math

import jax
import jax.numpy as jnp
from jax import lax
from jax.experimental import pallas as pl
from jax.experimental.pallas import tpu as pltpu
from jax.sharding import PartitionSpec as P

MESH = pl.DeviceIdType.MESH
F32 = jnp.float32
BF16 = jnp.bfloat16

LINES = 16
MEMBERS = 8
BLOCK = 512
HALF = 256
SPAN = MEMBERS * HALF
FEAT = 64
GATHERED = FEAT + 48
EMBED = 2560
INNER = 1024
COLS = 33
PROBE_ROWS = 48
SUM_ROWS = 40
PIECE = 1024
SUB = 512
NCHUNK = 256


def device_of(x, y, z, core):
    return ((z // 2) * 8 + y * 2 + core, x * 2 + z % 2)


def gelu(v):
    return 0.5 * v * (1.0 + lax.erf(v * (1.0 / math.sqrt(2.0))))


def pieces_of(v):
    first = v.astype(BF16).astype(F32)
    rest = v - first
    second = rest.astype(BF16).astype(F32)
    third = (rest - second).astype(BF16).astype(F32)
    return first, second, third


def kernel(
    emb, w_in, bias, w_out, scale_in, noise_in, rs_in,
    img_out, sc_out,
    x_buf, w_buf, b_buf, wo_buf, rs_buf, rs_pad, data, at, bb,
    acc_a, acc_b, parts, stat_own, stat_got,
    load_sem, ds_sem, dr_sem, qs_sem, qr_sem, ss_sem, sr_sem,
):
    row, col = lax.axis_index("row"), lax.axis_index("col")
    x, y, z, core = col // 2, (row // 2) % 4, (row // 8) * 2 + col % 2, row % 2
    line, member = y * 4 + z, x * 2 + core
    mates = []
    for dx, dc in ((2, 0), (2, 1), (1, 0), (1, 1), (3, 0), (3, 1), (0, 1)):
        mx, mc = (x + dx) % 4, (core + dc) % 2
        mates.append((mx * 2 + mc, device_of(mx, y, z, mc)))
    up = (line + member + 1) % LINES
    uy, uz = up // 4, up % 4
    uppers = [device_of(m // 2, uy, uz, m % 2) for m in range(MEMBERS)]
    lowers = []
    for m in range(MEMBERS):
        down = (line + LINES - 1 - m) % LINES
        lowers.append(device_of(m // 2, down // 4, down % 4, m % 2))
    across = []
    for d in range(1, LINES):
        there = ((y + d // 4) % 4, (z + d % 4) % 4)
        across.append((there[0] * 4 + there[1], device_of(x, there[0], there[1], core)))

    loads = []

    def load(src, dst):
        c = pltpu.make_async_copy(src, dst, load_sem.at[len(loads)])
        c.start()
        loads.append(c)
        return c

    chunks = INNER // NCHUNK
    load_rs = load(rs_in, rs_buf)
    load_x = [load(emb.at[pl.ds(0, HALF), :], x_buf.at[0])]
    load_w = [load(w_in.at[:, pl.ds(n * NCHUNK, NCHUNK)], w_buf.at[n]) for n in range(chunks)]
    load_b = load(bias, b_buf)
    load_wo = load(w_out, wo_buf)
    load_x.append(load(emb.at[pl.ds(HALF, HALF), :], x_buf.at[1]))

    barrier = pltpu.get_barrier_semaphore()
    partners = lowers + uppers + [d for _, d in mates + across]
    for device in partners:
        pl.semaphore_signal(barrier, inc=1, device_id=device, device_id_type=MESH)

    own = pl.ds(pl.multiple_of(member * HALF, HALF), HALF)

    def remote(src, dst, send, recv, device):
        return pltpu.make_async_remote_copy(
            src_ref=src, dst_ref=dst, send_sem=send, recv_sem=recv,
            device_id=device, device_id_type=MESH,
        )

    KINDS = ((0, FEAT, PROBE_ROWS), (0, 0, FEAT), (1, 0, GATHERED))

    def slot(place):
        return pl.ds(pl.multiple_of(place * HALF, HALF), HALF)

    def mate_copy(kind, i, receiving):
        half, start, count = KINDS[kind]
        place, device = mates[i]
        if not receiving:
            place = member
        return remote(
            data.at[2 + half, pl.ds(start, count), own],
            data.at[2 + half, pl.ds(start, count), slot(place)],
            ds_sem.at[kind, i], dr_sem.at[kind, place], device,
        )

    def column_copy(kind, m, receiving):
        half, start, count = KINDS[kind]
        place = m if receiving else member
        return remote(
            data.at[2 + half, pl.ds(start, count), own],
            data.at[half, pl.ds(start, count), slot(place)],
            ds_sem.at[kind, MEMBERS + m], dr_sem.at[kind, MEMBERS + place],
            uppers[m] if receiving else lowers[m],
        )

    def send_own(kind):
        for m in range(MEMBERS):
            column_copy(kind, m, False).start()
        for i in range(len(mates)):
            mate_copy(kind, i, False).start()

    def wait_rows(kind):
        for i in range(len(mates)):
            mate_copy(kind, i, True).wait_recv()

    def wait_columns(kind):
        for m in range(MEMBERS):
            column_copy(kind, m, True).wait_recv()

    load_rs.wait()
    rs_pad[...] = jnp.zeros_like(rs_pad)
    rs_pad[pl.ds(0, COLS), :] = rs_buf[...]
    for h in range(2):
        data[2 + h, pl.ds(FEAT, PROBE_ROWS), own] = rs_pad[:, pl.ds(h * HALF, HALF)].astype(BF16)
    acc_a[...] = jnp.zeros_like(acc_a)
    acc_b[...] = jnp.zeros_like(acc_b)

    for h in range(2):
        load_x[h].wait()
        total = jnp.zeros((FEAT, HALF), F32)
        for n in range(chunks):
            if h == 0:
                load_w[n].wait()
                if n == 0:
                    load_b.wait()
                    load_wo.wait()
            pre = jnp.dot(x_buf[h], w_buf[n], preferred_element_type=F32)
            hidden = gelu(pre + b_buf[:, pl.ds(n * NCHUNK, NCHUNK)]).astype(BF16)
            total += lax.dot_general(
                wo_buf[:, pl.ds(n * NCHUNK, NCHUNK)], hidden, (((1,), (1,)), ((), ())),
                preferred_element_type=F32,
            )
            if h == 0 and n == 0:
                pl.semaphore_wait(barrier, len(partners))
                send_own(0)
        data[2 + h, pl.ds(0, FEAT), own] = total.astype(BF16)
        send_own(1 + h)

    length = jnp.full((1, SPAN), scale_in[0], F32)
    unit = (1.0 / math.log(2.0)) / (length * length)
    level = lax.broadcasted_iota(jnp.int32, (FEAT, SPAN), 0)

    def extras(norm, at_norm, at_one):
        one, two, three = pieces_of(norm)
        out = jnp.where((level >= at_one) & (level < at_one + 3), 1.0, 0.0)
        for i, piece in enumerate((one, two, three)):
            out = jnp.where(level == at_norm + i, jnp.broadcast_to(piece, out.shape), out)
        return out

    def build_columns(half):
        wide = data[half, pl.ds(0, FEAT), :].astype(F32)
        norm = jnp.sum(wide * wide, axis=0, keepdims=True) * (unit * -0.5)
        for i, piece in enumerate(pieces_of(wide * unit)):
            bb[half, pl.ds(i * FEAT, FEAT), :] = piece.astype(BF16)
        bb[half, pl.ds(3 * FEAT, FEAT), :] = extras(norm, 0, 3).astype(BF16)

    def build_rows(h):
        wide = data[2 + h, pl.ds(0, FEAT), :].astype(F32)
        norm = jnp.sum(wide * wide, axis=0, keepdims=True) * (unit * -0.5)
        at[h, :, pl.ds(0, 128)] = jnp.concatenate([wide, wide], axis=0).T.astype(BF16)
        at[h, :, pl.ds(128, 128)] = jnp.concatenate([wide, extras(norm, 3, 0)], axis=0).T.astype(BF16)

    def strip(a, row0, rows, b, col0, cols, both=True):
        here = pl.ds(col0, cols)
        right = bb[b, :, here]
        down = jnp.zeros((PROBE_ROWS, cols), F32)
        for i in range(rows // SUB):
            part = pl.ds(row0 + i * SUB, SUB)
            power = jnp.dot(at[a, part, :], right, preferred_element_type=F32)
            tile = jnp.exp2(power).astype(BF16)
            down += jnp.dot(
                data[2 + a, pl.ds(FEAT, PROBE_ROWS), part], tile, preferred_element_type=F32
            )
            if both:
                acc_a[a, :, part] += lax.dot_general(
                    data[b, pl.ds(FEAT, PROBE_ROWS), here], tile,
                    (((1,), (1,)), ((), ())), preferred_element_type=F32,
                )
        acc_b[b, :, here] += down

    def quad(a, b, both=True):
        @pl.loop(0, SPAN // PIECE)
        def _(i):
            strip(a, 0, SPAN, b, pl.multiple_of(i * PIECE, PIECE), PIECE, both)

    special = member == MEMBERS - 1
    w = line // 8

    def row_part(half, m, receiving):
        place = m if receiving else member
        return remote(
            acc_a.at[half, pl.ds(0, SUM_ROWS), slot(m)], parts.at[half, place],
            qs_sem.at[half, m], qr_sem.at[half, place], device_of(m // 2, y, z, m % 2),
        )

    def column_part(half, m, receiving):
        place = MEMBERS + (m if receiving else member)
        device = lowers[m] if receiving else device_of(m // 2, uy, uz, m % 2)
        return remote(
            acc_b.at[half, pl.ds(0, SUM_ROWS), slot(m)], parts.at[half, place],
            qs_sem.at[half, MEMBERS + m], qr_sem.at[half, place], device,
        )

    def each_row_part(half, members, act):
        for m in members:
            @pl.when(member != m)
            def _():
                act(row_part(half, m, False))

    def each_column_part(half, members, act):
        for m in members:
            act(column_part(half, m, False))

    def start(c):
        c.start()

    def four(q):
        return [4 * q + i for i in range(4)]

    wait_rows(0)
    wait_rows(1)
    build_rows(0)

    @pl.when(special)
    def _():
        build_columns(2)
        quad(0, 2, False)

    wait_columns(0)
    wait_columns(1)
    build_columns(0)

    @pl.when(jnp.logical_not(special))
    def _():
        quad(0, 0)

    wait_rows(2)
    wait_columns(2)
    build_rows(1)
    build_columns(1)

    @pl.when(jnp.logical_not(special))
    def _():
        @pl.loop(0, 2)
        def _(q):
            at_piece = pl.multiple_of(q * PIECE, PIECE)
            strip(0, at_piece, PIECE, 1, 0, SPAN)
            each_row_part(0, four(q), start)
            strip(1, 0, SPAN, 0, at_piece, PIECE)
            each_column_part(0, four(q), start)

        strip(1, 0, PIECE, 1, 0, SPAN)
        each_row_part(1, four(0), start)

        @pl.loop(0, 2)
        def _(q):
            strip(1, PIECE, PIECE, 1, pl.multiple_of(q * PIECE, PIECE), PIECE)
            each_column_part(1, four(q), start)

        each_row_part(1, four(1), start)

    @pl.when(special)
    def _():
        quad(w, 0)
        each_column_part(0, range(MEMBERS), start)
        quad(1 - w, 1)
        each_column_part(1, range(MEMBERS), start)
        build_columns(3)
        quad(0, 3)
        acc_a[0] += acc_b[2]
        each_row_part(0, range(MEMBERS), start)
        quad(1, 3, False)
        acc_a[1] += acc_b[3]
        each_row_part(1, range(MEMBERS), start)

    for h in range(2):
        for m in range(MEMBERS):
            column_part(h, m, True).wait_recv()

            @pl.when(member != m)
            def _():
                row_part(h, m, True).wait_recv()

    right = [rs_pad[pl.ds(0, SUM_ROWS), pl.ds(h * HALF, HALF)] for h in range(2)]
    images = []
    for h in range(2):
        parts[h, member] = acc_a[h, pl.ds(0, SUM_ROWS), own]
        images.append(jnp.sum(parts[h], axis=0) + noise_in[0] * right[h])
        img_out[:, pl.ds(h * HALF, HALF)] = images[h][:COLS]

    def over(terms):
        return sum(jnp.sum(t, axis=1, keepdims=True) for t in terms)

    def ratio(top, bottom):
        return jnp.where(bottom > 0.0, top / jnp.where(bottom > 0.0, bottom, 1.0), 0.0)

    norm = over([r * r for r in right])
    curve = over([r * i for r, i in zip(right, images)])
    alpha = ratio(curve, norm)
    spread = over([(i - alpha * r) * (i - alpha * r) for r, i in zip(right, images)])
    lane = lax.broadcasted_iota(jnp.int32, (128, 128), 1)
    out = jnp.zeros((128, 128), F32)
    for i, v in enumerate((norm, curve, spread)):
        tall = jnp.concatenate([v, jnp.zeros((128 - SUM_ROWS, 1), F32)], axis=0)
        out = jnp.where(lane == i, jnp.broadcast_to(tall, out.shape), out)
    stat_own[0] = out.T[:8]

    level8 = lax.broadcasted_iota(jnp.int32, (8, 128), 0)

    def packed(values):
        out = jnp.zeros((8, 128), F32)
        for i, v in enumerate(values):
            out = jnp.where(level8 == i, jnp.broadcast_to(v, out.shape), out)
        return out

    def merged(stats):
        norms, curves, spreads = (stats[:, i : i + 1, :] for i in range(3))
        norm = jnp.sum(norms, axis=0)
        curve = jnp.sum(curves, axis=0)
        shift = ratio(curves, norms) - ratio(curve, norm)[None]
        return norm, curve, jnp.sum(spreads + norms * shift * shift, axis=0)

    stages = ((0, member, mates), (MEMBERS, line, across))

    def stat_copy(stage, i, receiving):
        base, mine, others = stages[stage]
        place, device = others[i]
        slot = base + (place if receiving else mine)
        return remote(
            stat_own.at[stage], stat_got.at[slot], ss_sem.at[base + i], sr_sem.at[slot], device
        )

    for stage, (base, mine, others) in enumerate(stages):
        for i in range(len(others)):
            stat_copy(stage, i, False).start()
        stat_got[base + mine] = stat_own[stage]
        for i in range(len(others)):
            stat_copy(stage, i, True).wait_recv()
        norm, curve, spread = merged(stat_got[pl.ds(base, len(others) + 1)])
        if stage < 1:
            stat_own[stage + 1] = packed((norm, curve, spread))
    step = norm / curve
    scalars = packed((step, step * step * spread / norm))
    sc_out[...] = jnp.concatenate([scalars, jnp.zeros((120, 128), F32)], axis=0).T[:COLS]

    def sent(c):
        c.wait_send()

    for kind in range(len(KINDS)):
        for i in range(len(mates)):
            mate_copy(kind, i, False).wait_send()
        for m in range(MEMBERS):
            column_copy(kind, m, False).wait_send()
    for h in range(2):
        each_row_part(h, range(MEMBERS), sent)
        each_column_part(h, range(MEMBERS), sent)
    for stage, (_, _, others) in enumerate(stages):
        for i in range(len(others)):
            stat_copy(stage, i, False).wait_send()


def on_device(embeddings, weight_in, bias_in, weight_out, lengthscale, noise_level, right_side):
    anywhere = pl.BlockSpec(memory_space=pl.ANY)
    scalar = pl.BlockSpec(memory_space=pltpu.SMEM)
    vmem = pl.BlockSpec(memory_space=pltpu.VMEM)
    dma = pltpu.SemaphoreType.DMA
    images, scalars = pl.pallas_call(
        kernel,
        out_shape=(
            jax.ShapeDtypeStruct((COLS, BLOCK), F32),
            jax.ShapeDtypeStruct((COLS, 128), F32),
        ),
        in_specs=[anywhere, anywhere, anywhere, anywhere, scalar, scalar, anywhere],
        out_specs=[vmem, vmem],
        scratch_shapes=[
            pltpu.VMEM((2, HALF, EMBED), BF16),
            pltpu.VMEM((INNER // NCHUNK, EMBED, NCHUNK), BF16),
            pltpu.VMEM((1, INNER), F32),
            pltpu.VMEM((FEAT, INNER), BF16),
            pltpu.VMEM((COLS, BLOCK), F32),
            pltpu.VMEM((PROBE_ROWS, BLOCK), F32),
            pltpu.VMEM((4, GATHERED, SPAN), BF16),
            pltpu.VMEM((2, SPAN, 256), BF16),
            pltpu.VMEM((4, 256, SPAN), BF16),
            pltpu.VMEM((2, PROBE_ROWS, SPAN), F32),
            pltpu.VMEM((4, PROBE_ROWS, SPAN), F32),
            pltpu.VMEM((2, 2 * MEMBERS, SUM_ROWS, HALF), F32),
            pltpu.VMEM((2, 8, 128), F32),
            pltpu.VMEM((MEMBERS + LINES, 8, 128), F32),
            dma((9,)),
            dma((3, 2 * MEMBERS)),
            dma((3, 2 * MEMBERS)),
            dma((2, 2 * MEMBERS)),
            dma((2, 2 * MEMBERS)),
            dma((MEMBERS + LINES,)),
            dma((MEMBERS + LINES,)),
        ],
        compiler_params=pltpu.CompilerParams(
            collective_id=0, has_side_effects=True, vmem_limit_bytes=56 * 2**20
        ),
        name="cg_step",
    )(
        embeddings, weight_in, bias_in.reshape(1, INNER), weight_out.T, lengthscale, noise_level,
        right_side,
    )
    step_size = scalars[:, 0]
    correction = scalars[:, 1]
    residual = right_side - step_size[:, None] * images
    direction = residual + correction[:, None] * right_side
    return (residual, direction, step_size, correction)


def solution(mesh):
    in_specs = (P(("row", "col"), None), P(), P(), P(), P(), P(), P(None, ("row", "col")))
    out_specs = (P(None, ("row", "col")), P(None, ("row", "col")), P(), P())
    return jax.shard_map(
        on_device, mesh=mesh, in_specs=in_specs, out_specs=out_specs, check_vma=False
    )
```

time: 595 us -> 78.2 us (0.13)
  waiting for transfers between devices: 319 us -> 0 us
  blocking collectives: 162 us -> 0 us
  Pallas kernels: 0 us -> 73.3 us
  matrix products: 71.2 us -> 0 us
  local copies, waits for them, and re-layouts: 22.1 us -> 1 us
  between operations: 15.5 us -> 2 us
    all_gather x1 -> x0, waiting for transfers between devices: 287 us -> none  [on_device(): all_feat = lax.all_gather(own_feat, ('row', 'col'), axis=1, tiled=True)]
    psum x2 -> x0, blocking collectives: 132 us -> none  [the longest x1 68 us: on_device(): norm_old = lax.psum(local_old, ('row', 'col'))]
    pallas_call x0 -> x1, Pallas kernels: none -> 73.3 us  [on_device(): pl.pallas_call(kernel, out_shape=(jax.ShapeDtypeStruct((COLS, BLOCK), F32...]
    dot_general x9 -> x0, matrix products: 71.2 us -> none  [the longest x8 60.9 us: tile_block(): lax.dot_general(cols_probe, kernel, (((1,), (1,)), ((), ())), preferred_e...]
    reduce_scatter x1 -> x0, waiting for transfers between devices: 32.2 us -> none  [on_device(): lax.psum_scatter(partial_products, 'col', scatter_dimension=1, tiled=True)]
    all_gather x1 -> x0, blocking collectives: 29.8 us -> none  [on_device(): cols_probe = lax.all_gather(probe_half, 'row', axis=1, tiled=True)]
    unnamed x18 -> x6, local copies, waits for them, and re-layouts: 14.6 us -> 0.02 us
    dynamic_slice x9 -> x0, local copies, waits for them, and re-layouts: 6.15 us -> none  [the longest x1 6.08 us: on_device(): lax.dynamic_index_in_dim(grid_feat, col_index, 2, keepdims=False)]
  transfers between devices with their start and end apart: 2 -> 0, of which waited for: 2 -> 0; matrix products, arithmetic and copies ran while one was open for 0% -> 0% of each run, Pallas kernels for 0% -> 0%
where the time goes in v2:
time: 78.2 us; the launch traced here: 78 us
  Pallas kernels  73.3 us (94%)
  between operations  2 us (3%)
  other arithmetic  1.63 us (2%)
  local copies, waits for them, and re-layouts  1 us (1%)
    pallas_call x1, Pallas kernels, on_device(): pl.pallas_call(kernel, out_shape=(jax.ShapeDtypeStruct((COLS, BLOCK), F32...  73.3 us
    add x1, other arithmetic, on_device(): direction = residual + correction[:, None] * right_side  1.63 us

profile of v2, /device:TPU:1, one launch (start us, length us, event | category | flops | bytes accessed | tf_op | source)
XLA Modules:
  0.0 78.0 jit_solution(6674393988886412493)
XLA Ops:
  0.6 0.0 copy-start
  2.0 73.3 %cg_step.1 = (f32[33,512]{1,0:T(8,128)}, f32[33,128]{1,0:T(8,128)}) custom-call(bf16[512,2560]{1,0:T(8,128)(2,1)} %emb.1, bf16[2560,1024]{1,0:T(8,128)(2,1)} %w_in.1, f32[1,1024]{1,0:T(1,128)} %bitcast.3, bf16[64,1024]{1,0:T(8,128)(2,1)} %bitcast.2, f32[1]{0:T(128)S(6)} %copy.11.scale_in, f32[1]{0:T(128)S(6)} %copy.12.noise_in, f32[33,512]{1,0:T(8,128)} %rs_in.1), custom_call_target="tpu_custom_call" | custom-call | tf_op jit(solution)/shard_map/cg_step/pallas_call | solution.py:400
  75.3 1.0 %slice_reduce_fusion = (f32[33]{0:T(128)S(1)}, f32[33]{0:T(128)S(1)}) fusion(f32[33,128]{1,0:T(8,128)} %get-tuple-element.6), kind=kLoop, calls=%fused_computation.2 | loop fusion | bytes 528 | tf_op jit(solution)/shard_map/slice | solution.py:440
  76.3 0.0 copy-start.1
  76.3 0.0 copy-start.2
  76.3 0.0 copy-done
  76.3 1.6 %multiply_add_fusion = (f32[33,512]{1,0:T(8,128)}, f32[33,512]{1,0:T(8,128)}) fusion(f32[33,512]{1,0:T(8,128)S(1)} %copy-done, f32[33]{0:T(128)S(1)} %get-tuple-element.8, f32[33,512]{1,0:T(8,128)} %get-tuple-element.7, f32[33]{0:T(128)S(1)} %get-tuple-element.9), kind=kLoop, calls=%fused_computation | loop fusion | flops 67584 | bytes 270600 | tf_op jit(solution)/shard_map/add | solution.py:442
  78.0 0.0 copy-done.1
  78.0 0.0 copy-done.2
Async XLA Ops:
  0.6 75.7 %copy-start = (f32[33,512]{1,0:T(8,128)S(1)}, f32[33,512]{1,0:T(8,128)}, u32[]{:S(2)}) copy-start(f32[33,512]{1,0:T(8,128)} %rs_in.1) | copy-start | bytes 202756
  76.3 1.7 %copy-start.1 = (f32[33]{0:T(128)}, f32[33]{0:T(128)S(1)}, u32[]{:S(2)}) copy-start(f32[33]{0:T(128)S(1)} %get-tuple-element.8) | copy-start | bytes 400
  76.3 1.7 %copy-start.2 = (f32[33]{0:T(128)}, f32[33]{0:T(128)S(1)}, u32[]{:S(2)}) copy-start(f32[33]{0:T(128)S(1)} %get-tuple-element.9) | copy-start | bytes 400

commit v3 on v2

--- a/solution.py
+++ b/solution.py
@@ -66,6 +66,14 @@
     for m in range(MEMBERS):
         down = (line + LINES - 1 - m) % LINES
         lowers.append(device_of(m // 2, down // 4, down % 4, m % 2))
+    targets = []
+    for dx in range(4):
+        tx = (x + dx) % 4
+        for tc in range(2):
+            down = (line + LINES - 1 - tx * 2 - tc) % LINES
+            targets.append(device_of(tx, down // 4, down % 4, tc))
+    sibling = device_of(x, y, z, 1 - core)
+    peers = [((x + dx) % 4, device_of((x + dx) % 4, y, z, core)) for dx in (2, 1, 3)]
     across = []
     for d in range(1, LINES):
         there = ((y + d // 4) % 4, (z + d % 4) % 4)
@@ -105,40 +113,54 @@
     def slot(place):
         return pl.ds(pl.multiple_of(place * HALF, HALF), HALF)
 
-    def mate_copy(kind, i, receiving):
+    def data_copy(kind, place, to_rows, send_at, device):
         half, start, count = KINDS[kind]
-        place, device = mates[i]
-        if not receiving:
-            place = member
+        rows = pl.ds(start, count)
         return remote(
-            data.at[2 + half, pl.ds(start, count), own],
-            data.at[2 + half, pl.ds(start, count), slot(place)],
-            ds_sem.at[kind, i], dr_sem.at[kind, place], device,
+            data.at[2 + half, rows, slot(place)],
+            data.at[half + (2 if to_rows else 0), rows, slot(place)],
+            ds_sem.at[kind, send_at],
+            dr_sem.at[kind, place if to_rows else MEMBERS + place], device,
         )
 
-    def column_copy(kind, m, receiving):
-        half, start, count = KINDS[kind]
-        place = m if receiving else member
-        return remote(
-            data.at[2 + half, pl.ds(start, count), own],
-            data.at[half, pl.ds(start, count), slot(place)],
-            ds_sem.at[kind, MEMBERS + m], dr_sem.at[kind, MEMBERS + place],
-            uppers[m] if receiving else lowers[m],
-        )
+    def own_copies(kind):
+        if kind == 2:
+            rows = [
+                data_copy(kind, member, True, 8 + i, device) for i, (_, device) in enumerate(mates)
+            ]
+            return rows + [data_copy(kind, member, False, i, targets[i]) for i in range(8)]
+        near = [data_copy(kind, member, False, i, targets[i]) for i in (4, 5, 2, 3, 6, 7, 0, 1)]
+        line_copies = [
+            data_copy(kind, member, True, 8 + i, device) for i, (_, device) in enumerate(peers)
+        ]
+        return line_copies + near + [data_copy(kind, member, True, 11, sibling)]
+
+    def passed_copies(kind, i):
+        place = peers[i][0] * 2 + core
+        copies = [data_copy(kind, place, True, 12 + i, sibling)]
+        return copies
 
     def send_own(kind):
-        for m in range(MEMBERS):
-            column_copy(kind, m, False).start()
-        for i in range(len(mates)):
-            mate_copy(kind, i, False).start()
+        for c in own_copies(kind):
+            c.start()
+
+    def pass_on(kind):
+        for i in range(len(peers)):
+            data_copy(kind, peers[i][0] * 2 + core, True, 8 + i, sibling).wait_recv()
+            for c in passed_copies(kind, i):
+                c.start()
 
     def wait_rows(kind):
-        for i in range(len(mates)):
-            mate_copy(kind, i, True).wait_recv()
+        if kind == 2:
+            for i, (place, device) in enumerate(mates):
+                data_copy(kind, place, True, 8 + i, device).wait_recv()
+            return
+        for dx in range(4):
+            data_copy(kind, (x + dx) % 4 * 2 + 1 - core, True, 11, sibling).wait_recv()
 
     def wait_columns(kind):
         for m in range(MEMBERS):
-            column_copy(kind, m, True).wait_recv()
+            data_copy(kind, m, False, m, uppers[m]).wait_recv()
 
     load_rs.wait()
     rs_pad[...] = jnp.zeros_like(rs_pad)
@@ -250,6 +272,8 @@
     def four(q):
         return [4 * q + i for i in range(4)]
 
+    pass_on(0)
+    pass_on(1)
     wait_rows(0)
     wait_rows(1)
     build_rows(0)
@@ -265,23 +289,29 @@
 
     @pl.when(jnp.logical_not(special))
     def _():
-        quad(0, 0)
+        strip(0, 0, SPAN, 0, 0, PIECE)
+
+    @pl.when(jnp.logical_not(special))
+    def _():
+        strip(0, 0, SPAN, 0, PIECE, PIECE)
 
     wait_rows(2)
+    build_rows(1)
+
+    @pl.when(jnp.logical_not(special))
+    def _():
+        for q in range(2):
+            strip(1, 0, SPAN, 0, q * PIECE, PIECE)
+            each_column_part(0, four(q), start)
+
     wait_columns(2)
-    build_rows(1)
     build_columns(1)
 
     @pl.when(jnp.logical_not(special))
     def _():
-        @pl.loop(0, 2)
-        def _(q):
-            at_piece = pl.multiple_of(q * PIECE, PIECE)
-            strip(0, at_piece, PIECE, 1, 0, SPAN)
+        for q in range(2):
+            strip(0, q * PIECE, PIECE, 1, 0, SPAN)
             each_row_part(0, four(q), start)
-            strip(1, 0, SPAN, 0, at_piece, PIECE)
-            each_column_part(0, four(q), start)
-
         strip(1, 0, PIECE, 1, 0, SPAN)
         each_row_part(1, four(0), start)
 
@@ -380,10 +410,10 @@
         c.wait_send()
 
     for kind in range(len(KINDS)):
-        for i in range(len(mates)):
-            mate_copy(kind, i, False).wait_send()
-        for m in range(MEMBERS):
-            column_copy(kind, m, False).wait_send()
+        for c in own_copies(kind) + (
+            sum((passed_copies(kind, i) for i in range(len(peers))), []) if kind < 2 else []
+        ):
+            c.wait_send()
     for h in range(2):
         each_row_part(h, range(MEMBERS), sent)
         each_column_part(h, range(MEMBERS), sent)

time: 78.2 us -> 76.3 us (0.976)
  Pallas kernels: 73.3 us -> 71.4 us
    pallas_call x1, Pallas kernels: 73.3 us -> 71.4 us  [on_device(): pl.pallas_call(kernel, out_shape=(jax.ShapeDtypeStruct((COLS, BLOCK), F32...]
where the time goes in v3:
time: 76.3 us; the launch traced here: 76 us
  Pallas kernels  71.4 us (94%)
  between operations  2 us (3%)
  other arithmetic  1.63 us (2%)
  local copies, waits for them, and re-layouts  1 us (1%)
    pallas_call x1, Pallas kernels, on_device(): pl.pallas_call(kernel, out_shape=(jax.ShapeDtypeStruct((COLS, BLOCK), F32...  71.4 us
    add x1, other arithmetic, on_device(): direction = residual + correction[:, None] * right_side  1.63 us

profile of v3, /device:TPU:1, one launch (start us, length us, event | category | flops | bytes accessed | tf_op | source)
XLA Modules:
  0.0 76.0 jit_solution(3140259886771317832)
XLA Ops:
  0.6 0.0 copy-start
  2.0 71.4 %cg_step.1 = (f32[33,512]{1,0:T(8,128)}, f32[33,128]{1,0:T(8,128)}) custom-call(bf16[512,2560]{1,0:T(8,128)(2,1)} %emb.1, bf16[2560,1024]{1,0:T(8,128)(2,1)} %w_in.1, f32[1,1024]{1,0:T(1,128)} %bitcast.3, bf16[64,1024]{1,0:T(8,128)(2,1)} %bitcast.2, f32[1]{0:T(128)S(6)} %copy.11.scale_in, f32[1]{0:T(128)S(6)} %copy.12.noise_in, f32[33,512]{1,0:T(8,128)} %rs_in.1), custom_call_target="tpu_custom_call" | custom-call | tf_op jit(solution)/shard_map/cg_step/pallas_call | solution.py:430
  73.4 1.0 %slice_reduce_fusion = (f32[33]{0:T(128)S(1)}, f32[33]{0:T(128)S(1)}) fusion(f32[33,128]{1,0:T(8,128)} %get-tuple-element.6), kind=kLoop, calls=%fused_computation.2 | loop fusion | bytes 528 | tf_op jit(solution)/shard_map/slice | solution.py:470
  74.4 0.0 copy-start.1
  74.4 0.0 copy-start.2
  74.4 0.0 copy-done
  74.4 1.6 %multiply_add_fusion = (f32[33,512]{1,0:T(8,128)}, f32[33,512]{1,0:T(8,128)}) fusion(f32[33,512]{1,0:T(8,128)S(1)} %copy-done, f32[33]{0:T(128)S(1)} %get-tuple-element.8, f32[33,512]{1,0:T(8,128)} %get-tuple-element.7, f32[33]{0:T(128)S(1)} %get-tuple-element.9), kind=kLoop, calls=%fused_computation | loop fusion | flops 67584 | bytes 270600 | tf_op jit(solution)/shard_map/add | solution.py:472
  76.0 0.0 copy-done.1
  76.0 0.0 copy-done.2
Async XLA Ops:
  0.6 73.8 %copy-start = (f32[33,512]{1,0:T(8,128)S(1)}, f32[33,512]{1,0:T(8,128)}, u32[]{:S(2)}) copy-start(f32[33,512]{1,0:T(8,128)} %rs_in.1) | copy-start | bytes 202756
  74.4 1.7 %copy-start.1 = (f32[33]{0:T(128)}, f32[33]{0:T(128)S(1)}, u32[]{:S(2)}) copy-start(f32[33]{0:T(128)S(1)} %get-tuple-element.8) | copy-start | bytes 400
  74.4 1.7 %copy-start.2 = (f32[33]{0:T(128)}, f32[33]{0:T(128)S(1)}, u32[]{:S(2)}) copy-start(f32[33]{0:T(128)S(1)} %get-tuple-element.9) | copy-start | bytes 400

commit v4 on v3

--- a/solution.py
+++ b/solution.py
@@ -289,28 +289,26 @@
 
     @pl.when(jnp.logical_not(special))
     def _():
-        strip(0, 0, SPAN, 0, 0, PIECE)
+        quad(0, 0)
+
+    wait_rows(2)
+    build_rows(1)
 
     @pl.when(jnp.logical_not(special))
     def _():
-        strip(0, 0, SPAN, 0, PIECE, PIECE)
-
-    wait_rows(2)
-    build_rows(1)
+        @pl.loop(0, 2)
+        def _(q):
+            strip(1, 0, SPAN, 0, pl.multiple_of(q * PIECE, PIECE), PIECE)
+            each_column_part(0, four(q), start)
+
+    wait_columns(2)
+    build_columns(1)
 
     @pl.when(jnp.logical_not(special))
     def _():
-        for q in range(2):
-            strip(1, 0, SPAN, 0, q * PIECE, PIECE)
-            each_column_part(0, four(q), start)
-
-    wait_columns(2)
-    build_columns(1)
-
-    @pl.when(jnp.logical_not(special))
-    def _():
-        for q in range(2):
-            strip(0, q * PIECE, PIECE, 1, 0, SPAN)
+        @pl.loop(0, 2)
+        def _(q):
+            strip(0, pl.multiple_of(q * PIECE, PIECE), PIECE, 1, 0, SPAN)
             each_row_part(0, four(q), start)
         strip(1, 0, PIECE, 1, 0, SPAN)
         each_row_part(1, four(0), start)

time: 76.3 us -> 76.2 us (level)
  no operation moved by 1% of the time
where the time goes in v4:
time: 76.2 us; the launch traced here: 75.9 us
  Pallas kernels  71.3 us (94%)
  between operations  2 us (3%)
  other arithmetic  1.63 us (2%)
  local copies, waits for them, and re-layouts  1 us (1%)
    pallas_call x1, Pallas kernels, on_device(): pl.pallas_call(kernel, out_shape=(jax.ShapeDtypeStruct((COLS, BLOCK), F32...  71.3 us
    add x1, other arithmetic, on_device(): direction = residual + correction[:, None] * right_side  1.63 us

profile of v4, /device:TPU:1, one launch (start us, length us, event | category | flops | bytes accessed | tf_op | source)
XLA Modules:
  0.0 75.9 jit_solution(11612287461608799940)
XLA Ops:
  0.6 0.0 copy-start
  2.0 71.3 %cg_step.1 = (f32[33,512]{1,0:T(8,128)}, f32[33,128]{1,0:T(8,128)}) custom-call(bf16[512,2560]{1,0:T(8,128)(2,1)} %emb.1, bf16[2560,1024]{1,0:T(8,128)(2,1)} %w_in.1, f32[1,1024]{1,0:T(1,128)} %bitcast.3, bf16[64,1024]{1,0:T(8,128)(2,1)} %bitcast.2, f32[1]{0:T(128)S(6)} %copy.11.scale_in, f32[1]{0:T(128)S(6)} %copy.12.noise_in, f32[33,512]{1,0:T(8,128)} %rs_in.1), custom_call_target="tpu_custom_call" | custom-call | tf_op jit(solution)/shard_map/cg_step/pallas_call | solution.py:428
  73.3 1.0 %slice_reduce_fusion = (f32[33]{0:T(128)S(1)}, f32[33]{0:T(128)S(1)}) fusion(f32[33,128]{1,0:T(8,128)} %get-tuple-element.6), kind=kLoop, calls=%fused_computation.2 | loop fusion | bytes 528 | tf_op jit(solution)/shard_map/slice | solution.py:468
  74.3 0.0 copy-start.1
  74.3 0.0 copy-start.2
  74.3 0.0 copy-done
  74.3 1.6 %multiply_add_fusion = (f32[33,512]{1,0:T(8,128)}, f32[33,512]{1,0:T(8,128)}) fusion(f32[33,512]{1,0:T(8,128)S(1)} %copy-done, f32[33]{0:T(128)S(1)} %get-tuple-element.8, f32[33,512]{1,0:T(8,128)} %get-tuple-element.7, f32[33]{0:T(128)S(1)} %get-tuple-element.9), kind=kLoop, calls=%fused_computation | loop fusion | flops 67584 | bytes 270600 | tf_op jit(solution)/shard_map/add | solution.py:470
  75.9 0.0 copy-done.1
  75.9 0.0 copy-done.2
Async XLA Ops:
  0.6 73.7 %copy-start = (f32[33,512]{1,0:T(8,128)S(1)}, f32[33,512]{1,0:T(8,128)}, u32[]{:S(2)}) copy-start(f32[33,512]{1,0:T(8,128)} %rs_in.1) | copy-start | bytes 202756
  74.3 1.7 %copy-start.1 = (f32[33]{0:T(128)}, f32[33]{0:T(128)S(1)}, u32[]{:S(2)}) copy-start(f32[33]{0:T(128)S(1)} %get-tuple-element.8) | copy-start | bytes 400
  74.3 1.7 %copy-start.2 = (f32[33]{0:T(128)}, f32[33]{0:T(128)S(1)}, u32[]{:S(2)}) copy-start(f32[33]{0:T(128)S(1)} %get-tuple-element.9) | copy-start | bytes 400
